TPU v7x, 32 devices: a whole 2x2x4 slice. The times are simulated.
32 devices in a mesh: sector: 2 (over y), cell: 16 (over z, x, core).
Axes of the slice: x: 2, y: 2, z: 4, core: 2. Of those that a mesh axis runs over, the one named last changes fastest.
Arguments:
- fluid: bfloat16 [2048, 320], P(('sector', 'cell')), may hold values from -10 to 10, as said below
- bead_vel: float32 [512, 3, 128], P(('sector', 'cell')), may hold values from -6 to 6
- bead_diam: float32 [512, 128], P(('sector', 'cell')), may hold values from 0.5 to 2
- weights: bfloat16 [512, 8, 64, 128], P(('sector', 'cell')), may hold values from 0.002 to 1.002, as said below
- tile_owner: int32 [512, 8], P(('sector', 'cell')), may hold values from 0 to 17, all different within a row; in each aligned block of 16 rows (0 to 15, 16 to 31, ...) at most 15 rows name the same one
- tile_local: int32 [512, 8], P(('sector', 'cell')), may hold values from 0 to 63
- tile_count: int32 [512], P(('sector', 'cell')), may hold values from 1 to 8
Outputs:
- bead_drag: float32 [512, 3, 128], P(('sector', 'cell'))
- cell_source: float32 [2048, 192], P(('sector', 'cell'))
Inputs may be any that keep to these rules, and one draw needn't show every extreme that they name: `tile_owner`: each row names 8 different owners: below 16 the device of that cell index in the bead block's own angular group, 16 the device of the same cell index in the previous angular group, 17 that in the next (groups wrap around). Among the bead blocks of one device no owner is named by more than 15 rows, a bound that some block reaches. Fields 0 to 2 of each row are velocity components, field 3 the fluid volume fraction in 0.4 to 0.95, field 4 the viscosity in 0.05 to 0.5. Nonnegative kernel weights, each at least 0.002.
All inputs are finite; a program needn't handle non-finite values.
Results may differ from a plain program's by a relative error of at most 0.0023.
Values may be sent and summed in bfloat16 or wider, within the bound.
A program may use at most 64 MiB of HBM per device.

v0:
```python
import jax
import jax.numpy as jnp
from jax import lax
from jax.sharding import PartitionSpec as P

FIELDS = 5


def padded(block, sides, width):
    for axis, dim in sides:
        count = lax.axis_size(axis)
        forward = [(i, i + 1) for i in range(count - 1)]
        forward.append((count - 1, 0))
        backward = [(target, source) for source, target in forward]
        low = lax.ppermute(
            lax.slice_in_dim(block, block.shape[dim] - width, None, axis=dim), axis, forward
        )
        high = lax.ppermute(lax.slice_in_dim(block, 0, width, axis=dim), axis, backward)
        block = jnp.concatenate([low, block, high], axis=dim)
    return block


def local(fluid, bead_vel, bead_diam, weights, tile_owner, tile_local, tile_count):
    ncell = lax.axis_size("cell")
    blocks_dev = fluid.shape[0]
    bead_blocks = weights.shape[0]
    lists = weights.shape[1]
    cells_block = weights.shape[2]
    owner_flat = tile_owner.reshape(-1)
    local_flat = tile_local.reshape(-1)
    live_mask = (jnp.arange(lists)[None, :] < tile_count[:, None]).astype(jnp.float32)
    in_group = owner_flat < ncell
    rim_pick = jnp.clip(owner_flat - ncell, 0, 1)
    rims_fluid = padded(fluid, (("sector", 0),), blocks_dev)
    rim_table = jnp.concatenate([rims_fluid[:blocks_dev], rims_fluid[2 * blocks_dev :]], axis=0)
    rim_rows = rim_table[rim_pick * blocks_dev + local_flat]
    table = lax.all_gather(fluid, "cell", axis=0, tiled=True)
    group_rows = table[jnp.minimum(owner_flat, ncell - 1) * blocks_dev + local_flat]
    tile_fluid = jnp.where(in_group[:, None], group_rows, rim_rows)
    fluid_tiles = tile_fluid.reshape(bead_blocks, lists, FIELDS, cells_block)
    tile_vals = jnp.einsum(
        "bkfc,bkcn->bkfn", fluid_tiles, weights, preferred_element_type=jnp.float32
    )
    weight_sums = jnp.sum(weights, axis=2, dtype=jnp.float32)
    weight_total = jnp.sum(live_mask[:, :, None] * weight_sums, axis=1)
    interp = jnp.sum(live_mask[:, :, None, None] * tile_vals, axis=1) / weight_total[:, None, :]
    slip_vel = interp[:, 0:3] - bead_vel
    porosity = interp[:, 3]
    viscosity = interp[:, 4]
    slip_speed = jnp.sqrt(jnp.sum(slip_vel * slip_vel, axis=1) + 0.01)
    reynolds = porosity * bead_diam * slip_speed / viscosity
    drag_coef = (
        viscosity
        * (1.0 + 0.15 * jnp.power(reynolds, 0.687))
        * jnp.power(porosity, -1.65)
        / (bead_diam * bead_diam)
    )
    bead_drag = drag_coef[:, None, :] * slip_vel
    scaled_drag = (bead_drag / weight_total[:, None, :]).astype(jnp.bfloat16)
    partials = jnp.einsum(
        "bkcn,bjn->bkjc", weights, scaled_drag, preferred_element_type=jnp.float32
    )
    partials = (-live_mask[:, :, None, None] * partials).reshape(
        bead_blocks * lists, 3 * cells_block
    )
    group_ids = jnp.where(in_group, owner_flat * blocks_dev + local_flat, -1)
    selector = (
        group_ids[None, :] == jnp.arange(blocks_dev * lax.axis_size("cell"))[:, None]
    ).astype(jnp.float32)
    own_source = lax.psum_scatter(
        jnp.dot(
            selector, partials, precision=lax.Precision.HIGHEST, preferred_element_type=jnp.float32
        ),
        "cell",
        scatter_dimension=0,
        tiled=True,
    )
    rim_ids = jnp.where(in_group, -1, (owner_flat - ncell) * blocks_dev + local_flat)
    rim_selector = (rim_ids[None, :] == jnp.arange(2 * blocks_dev)[:, None]).astype(jnp.float32)
    rim_parts = jnp.dot(
        rim_selector, partials, precision=lax.Precision.HIGHEST, preferred_element_type=jnp.float32
    )
    rim_in = padded(rim_parts, (("sector", 0),), blocks_dev)
    rim_source = rim_in[:blocks_dev] + rim_in[3 * blocks_dev :]
    cell_source = own_source + rim_source
    return (bead_drag, cell_source)


def solution(mesh):
    in_specs = (
        P(("sector", "cell"), None),
        P(("sector", "cell"), None, None),
        P(("sector", "cell"), None),
        P(("sector", "cell"), None, None, None),
        P(("sector", "cell"), None),
        P(("sector", "cell"), None),
        P(("sector", "cell")),
    )
    out_specs = (P(("sector", "cell"), None, None), P(("sector", "cell"), None))
    return jax.shard_map(local, mesh=mesh, in_specs=in_specs, out_specs=out_specs, check_vma=False)
```

profile of v0, /device:TPU:0, one launch (start us, length us, event | category | flops | bytes accessed | tf_op | source)
XLA Modules:
  0.0 110.6 jit_solution(16357344343589314241)
XLA Ops:
  7.2 3.0 %collective-permute-start.1 = (bf16[64,320]{1,0:T(8,128)(2,1)}, bf16[64,320]{1,0:T(8,128)(2,1)S(1)}, u32[]{:S(2)}, u32[]{:S(2)}) collective-permute-start(bf16[64,320]{1,0:T(8,128)(2,1)} %param.7), channel_id=1, source_target_pairs={{16,0},{0,16},{17,1},{1,17},{18,2},{2,18},{19,3},{3,19},{20,4},{4,... | collective-permute-start | bytes 122888 | tf_op jit(solution)/shard_map/ppermute | solution.py:18
  10.2 0.1 collective-permute-start
  10.3 24.6 %all_gather.3 = bf16[1024,320]{1,0:T(8,128)(2,1)S(1)} all-gather(bf16[64,320]{1,0:T(8,128)(2,1)} %param.7), channel_id=1, replica_groups=mesh['sector'=2,'cell'=16] {'cell'}, dimensions={0}, use_global_device_ids=true | all-gather | bytes 696320 | tf_op jit(solution)/shard_map/all_gather | solution.py:37
  34.9 0.7 fusion.9
  35.6 0.7 fusion.10
  36.3 0.7 broadcast_compare_fusion
  37.0 0.7 add_select_fusion
  37.8 0.1 add.103
  37.9 0.1 copy.37
  38.0 0.1 add.107
  38.1 2.4 %convert_reduce_fusion = f32[16,8,128]{2,1,0:T(8,128)S(1)} fusion(bf16[16,8,64,128]{3,2,1,0:T(8,128)(2,1)} %param.10), kind=kLoop, calls=%fused_computation.2 | loop fusion | flops 2080768 | bytes 2162688 | tf_op jit(solution)/shard_map/reduce_sum | solution.py:44
  40.5 0.1 multiply_reduce_fusion
  40.6 0.9 gather_fusion
  41.5 0.2 gather.11
  41.6 0.1 copy.35
  41.8 0.1 select_n.51
  42.0 0.9 gather_fusion.1
  42.8 0.2 gather.13
  43.0 0.7 fusion
  43.9 1.7 %fusion.1 = f32[16,8,3,64]{3,2,1,0:T(4,128)S(1)} fusion(bf16[16,8,64,128]{3,2,1,0:T(8,128)(2,1)S(1)} %copy-done, f32[16,8]{1,0:T(8,128)S(1)} %fusion.10, f32[16,3,128]{2,1,0:T(4,128)S(1)} %broadcast_multiply_fusion, f32[16,128]{1,0:T(8,128)S(1)} %multiply_reduce_fusion), kind=kOutput, calls=%fused_computation.6 | convolution fusion | flops 6328320 | bytes 2228736 | tf_op jit(solution)/shard_map/bkcn,bjn->bkjc/dot_general | solution.py:60
  45.6 0.2 reshape.207
  45.8 1.6 %fusion.2 = f32[1024,192]{1,0:T(8,128)} fusion(f32[128,192]{1,0:T(8,128)S(1)} %reshape.207, s32[128]{0:T(128)S(1)} %select_n.51), kind=kOutput, calls=%fused_computation.8 | convolution fusion | flops 302120960 | bytes 885248 | tf_op jit(solution)/shard_map/dot_general | solution.py:71
  47.4 0.1 copy.41
  47.5 0.1 select_n.53
  47.6 0.2 fusion.6
  47.8 1.6 %collective-permute-start.2 = (f32[64,192]{1,0:T(8,128)S(1)}, f32[64,192]{1,0:T(8,128)S(1)}, u32[]{:S(2)}, u32[]{:S(2)}) collective-permute-start(f32[64,192]{1,0:T(8,128)S(1)} %get-tuple-element.7), channel_id=1, source_target_pairs={{0,16},{16,0},{1,17},{17,1},{2,18},{18,2},{3,19},{19,3},{4,20},{20... | collective-permute-start | bytes 147464 | tf_op jit(solution)/shard_map/ppermute | solution.py:15
  49.4 0.5 collective-permute-start.3
  49.9 0.6 copy.44
  50.5 1.9 %collective-permute-done.2 = f32[64,192]{1,0:T(8,128)S(1)} collective-permute-done((f32[64,192]{1,0:T(8,128)S(1)}, f32[64,192]{1,0:T(8,128)S(1)}, u32[]{:S(2)}, u32[]{:S(2)}) %collective-permute-start.2) | collective-permute-done | bytes 49184 | tf_op jit(solution)/shard_map/ppermute | solution.py:15
  52.5 1.2 %collective-permute-done.3 = f32[64,192]{1,0:T(8,128)S(1)} collective-permute-done((f32[64,192]{1,0:T(8,128)S(1)}, f32[64,192]{1,0:T(8,128)S(1)}, u32[]{:S(2)}, u32[]{:S(2)}) %collective-permute-start.3) | collective-permute-done | bytes 49184 | tf_op jit(solution)/shard_map/ppermute | solution.py:18
  53.7 48.6 %reduce-scatter.2.cloned.1.call-done = f32[64,192]{1,0:T(8,128)} async-done(((f32[1024,192]{1,0:T(8,128)}), f32[64,192]{1,0:T(8,128)}) %reduce-scatter.2.cloned.1.call-update) | async-done | bytes 49168 | tf_op jit(solution)/shard_map/reduce_scatter | solution.py:70
  102.3 1.5 %add_add_fusion = f32[64,192]{1,0:T(8,128)} fusion(f32[64,192]{1,0:T(8,128)} %reduce-scatter.2.cloned.1.call-done, f32[64,192]{1,0:T(8,128)S(1)} %collective-permute-done.2, f32[64,192]{1,0:T(8,128)S(1)} %collective-permute-done.3), kind=kLoop, calls=%fused_computation.13 | loop fusion | flops 24576 | bytes 196608 | tf_op jit(solution)/shard_map/add | solution.py:85
  (23 shorter events, 0.4 us)
Async XLA Ops:
  7.2 95.1 %reduce-scatter.2.cloned.1.call-start = ((), (), s32[]{:S(2)}) async-start(), calls=%async_computation.1 | async-start | bytes 1114112 | tf_op jit(solution)/shard_map/reduce_scatter | solution.py:70
  7.2 34.7 %collective-permute-start.1 = (bf16[64,320]{1,0:T(8,128)(2,1)}, bf16[64,320]{1,0:T(8,128)(2,1)S(1)}, u32[]{:S(2)}, u32[]{:S(2)}) collective-permute-start(bf16[64,320]{1,0:T(8,128)(2,1)} %param.7), channel_id=1, source_target_pairs={{16,0},{0,16},{17,1},{1,17},{18,2},{2,18},{19,3},{3,19},{20,4},{4,... | collective-permute-start | bytes 122888 | tf_op jit(solution)/shard_map/ppermute | solution.py:18
  10.2 31.7 %collective-permute-start = (bf16[64,320]{1,0:T(8,128)(2,1)}, bf16[64,320]{1,0:T(8,128)(2,1)S(1)}, u32[]{:S(2)}, u32[]{:S(2)}) collective-permute-start(bf16[64,320]{1,0:T(8,128)(2,1)} %param.7), channel_id=1, source_target_pairs={{0,16},{16,0},{1,17},{17,1},{2,18},{18,2},{3,19},{19,3},{4,20},{20... | collective-permute-start | bytes 122888 | tf_op jit(solution)/shard_map/ppermute | solution.py:15
  38.1 4.9 %copy-start = (bf16[16,8,64,128]{3,2,1,0:T(8,128)(2,1)S(1)}, bf16[16,8,64,128]{3,2,1,0:T(8,128)(2,1)}, u32[]{:S(2)}) copy-start(bf16[16,8,64,128]{3,2,1,0:T(8,128)(2,1)} %param.10) | copy-start | bytes 6291460
  41.9 1.8 %copy-start.1 = (f32[16,3,128]{2,0,1:T(8,128)S(1)}, f32[16,3,128]{2,0,1:T(8,128)}, u32[]{:S(2)}) copy-start(f32[16,3,128]{2,0,1:T(8,128)} %param.8) | copy-start | bytes 73732
  41.9 1.9 %copy-start.2 = (f32[16,128]{1,0:T(8,128)S(1)}, f32[16,128]{1,0:T(8,128)}, u32[]{:S(2)}) copy-start(f32[16,128]{1,0:T(8,128)} %param.9) | copy-start | bytes 24580
  47.8 4.6 %collective-permute-start.2 = (f32[64,192]{1,0:T(8,128)S(1)}, f32[64,192]{1,0:T(8,128)S(1)}, u32[]{:S(2)}, u32[]{:S(2)}) collective-permute-start(f32[64,192]{1,0:T(8,128)S(1)} %get-tuple-element.7), channel_id=1, source_target_pairs={{0,16},{16,0},{1,17},{17,1},{2,18},{18,2},{3,19},{19,3},{4,20},{20... | collective-permute-start | bytes 147464 | tf_op jit(solution)/shard_map/ppermute | solution.py:15
  49.4 4.3 %collective-permute-start.3 = (f32[64,192]{1,0:T(8,128)S(1)}, f32[64,192]{1,0:T(8,128)S(1)}, u32[]{:S(2)}, u32[]{:S(2)}) collective-permute-start(f32[64,192]{1,0:T(8,128)S(1)} %get-tuple-element.6), channel_id=1, source_target_pairs={{16,0},{0,16},{17,1},{1,17},{18,2},{2,18},{19,3},{3,19},{20,4},{4,... | collective-permute-start | bytes 147464 | tf_op jit(solution)/shard_map/ppermute | solution.py:18
Sparse Core Ops, SparseCore 0:
  47.6 54.6 reduce-scatter.1
where the time goes:
time: 111 us
  waiting for transfers between devices  51.8 us (47%)
  blocking collectives  24.6 us (22%)
  between operations  14.2 us (13%)
  other arithmetic  6.96 us (6%)
  starting transfers between devices  5.24 us (5%)
  matrix products  4.25 us (4%)
  local copies, waits for them, and re-layouts  3.61 us (3%)
    reduce_scatter x1, waiting for transfers between devices, local(): lax.psum_scatter(jnp.dot(selector, partials, precision=lax.Precision.HIGH...  48.6 us
    all_gather x1, blocking collectives, local(): table = lax.all_gather(fluid, 'cell', axis=0, tiled=True)  24.6 us
    ppermute x2, starting transfers between devices, padded(): lax.ppermute(lax.slice_in_dim(block, 0, width, axis=dim), axis, backward)  3.54 us
    reduce_sum x1, other arithmetic, local(): weight_sums = jnp.sum(weights, axis=2, dtype=jnp.float32)  2.39 us
  transfers between devices with their start and end apart: 5, of which 3 were waited for; matrix products, arithmetic and copies ran while one was open for 7% of the time, Pallas kernels for 0%

commit v1 on v0

v1 whole, which is shorter than its diff:
```python
import functools

import jax
import jax.numpy as jnp
from jax import lax
from jax.experimental import pallas as pl
from jax.experimental.pallas import tpu as pltpu
from jax.sharding import PartitionSpec as P

FIELDS = 5
MESH = pl.DeviceIdType.MESH


def kernel(
    nsec, ncell, fluid_ref, vel_ref, diam_ref, weights_ref, owner_ref, local_ref, count_ref,
    drag_ref, source_ref,
    w, table, ask, asked, asked_t, reply, rows, lhs, mixed, scaled, parts, give, got,
    w_sem, ask_send, ask_recv, reply_send, reply_recv, give_send, give_recv,
):
    lists = owner_ref.shape[1]
    beads = owner_ref.shape[0]
    cells = fluid_ref.shape[0]
    slots = ncell + 2
    f32, bf16 = jnp.float32, jnp.bfloat16
    me = lax.axis_index("cell")
    sec = lax.axis_index("sector")
    prev = {"sector": lax.rem(sec + nsec - 1, nsec)}
    succ = {"sector": lax.rem(sec + 1, nsec)}
    around = [lax.rem(me + t, ncell) for t in range(1, ncell)]
    to_owner = [(ncell, prev, ncell), (ncell + 1, succ, ncell + 1)]
    to_owner += [(o, {"cell": o}, me) for o in around]
    to_asker = [(ncell, succ, ncell), (ncell + 1, prev, ncell + 1)]
    to_asker += [(o, {"cell": o}, me) for o in around]

    barrier = pltpu.get_barrier_semaphore()
    for _, device, _ in to_owner:
        pl.semaphore_signal(barrier, inc=1, device_id=device, device_id_type=MESH)

    load_w = pltpu.make_async_copy(weights_ref, w, w_sem)
    load_w.start()

    def copy(src, dst, here, device, there, send, recv):
        return pltpu.make_async_remote_copy(
            src_ref=src.at[here], dst_ref=dst.at[there], send_sem=send.at[here],
            recv_sem=recv.at[there], device_id=device, device_id_type=MESH,
        )

    def arrived(src, dst, send, recv, links):
        for slot, device, _ in links:
            copy(src, dst, slot, device, slot, send, recv).wait_recv()

    lane = lax.broadcasted_iota(jnp.int32, (beads, 128), 1)
    square = (beads, beads)
    diagonal = lax.broadcasted_iota(jnp.int32, square, 0) == lax.broadcasted_iota(jnp.int32, square, 1)
    counts = jnp.broadcast_to(count_ref[...].astype(f32), square)
    counts = jnp.sum(jnp.where(diagonal, counts, 0.0), axis=1, keepdims=True)
    turn = lax.broadcasted_iota(jnp.int32, (beads, lists), 1).astype(f32)
    live = turn < counts
    keys = jnp.where(live, owner_ref[...] * 128 + local_ref[...], -1)
    owners = jnp.where(live, owner_ref[...], -1)
    key_of = [jnp.broadcast_to(keys[:, k : k + 1], (beads, 128)) for k in range(lists)]
    owner_of = [jnp.broadcast_to(owners[:, k : k + 1], (beads, 128)) for k in range(lists)]

    for o in range(slots):
        hit = key_of[0] == lane + o * 128
        for k in range(1, lists):
            hit = hit | (key_of[k] == lane + o * 128)
        ask[o] = jnp.where(hit, 1.0, 0.0).astype(bf16)

    pl.semaphore_wait(barrier, len(to_owner))
    asks = [copy(ask, asked, h, d, t, ask_send, ask_recv) for h, d, t in to_owner]
    for c in asks:
        c.start()
    asked[pl.ds(me, 1)] = ask[pl.ds(me, 1)]
    table[...] = jnp.ones_like(table)
    table[:, : FIELDS * cells] = fluid_ref[...]
    lhs[...] = jnp.zeros_like(lhs)
    scaled[...] = jnp.zeros_like(scaled)

    arrived(ask, asked, ask_send, ask_recv, to_owner)
    wanted = asked[...].reshape(slots * beads, 128)
    picked = jnp.dot(wanted[:, :cells], table[...], preferred_element_type=f32)
    reply[...] = picked.astype(bf16).reshape(reply.shape)
    replies = [copy(reply, rows, h, d, t, reply_send, reply_recv) for h, d, t in to_asker]
    for c in replies:
        c.start()
    rows[pl.ds(me, 1)] = reply[pl.ds(me, 1)]
    asked_t[...] = wanted.astype(f32).T.astype(bf16)
    load_w.wait()
    arrived(reply, rows, reply_send, reply_recv, to_asker)

    low = lane < 64
    for c in range(3):
        held = [jnp.zeros((beads, 128), f32) for _ in range(lists)]
        for o in range(slots):
            row = rows[o, :, c * 128 : (c + 1) * 128].astype(f32)
            held = [jnp.where(owner_of[k] == o, row, held[k]) for k in range(lists)]
        for m in range(lists // 2):
            one, two = held[2 * m], held[2 * m + 1]
            even = jnp.where(low, one, pltpu.roll(two, 64, 1))
            odd = jnp.where(low, pltpu.roll(one, 64, 1), two)
            lhs[m, pl.ds(2 * c, beads, stride=8), :] = even
            lhs[m, pl.ds(2 * c + 1, beads, stride=8), :] = odd

    for b in range(beads):
        eight = slice(b * 8, (b + 1) * 8)
        left = jnp.concatenate([lhs[m, eight, :] for m in range(lists // 2)], axis=1)
        mixed[eight, :] = jnp.dot(left.astype(bf16), w[b], preferred_element_type=f32)

    field = [mixed[pl.ds(f, beads, stride=8), :] for f in range(FIELDS + 1)]
    total = field[FIELDS]
    interp = [field[f] / total for f in range(FIELDS)]
    slip = [interp[i] - vel_ref[:, i, :] for i in range(3)]
    porosity, viscosity = interp[3], interp[4]
    diam = diam_ref[...]
    speed = jnp.sqrt(slip[0] * slip[0] + slip[1] * slip[1] + slip[2] * slip[2] + 0.01)
    reynolds = porosity * diam * speed / viscosity
    coef = (
        viscosity
        * (1.0 + 0.15 * jnp.exp(0.687 * jnp.log(reynolds)))
        * jnp.exp(-1.65 * jnp.log(porosity))
        / (diam * diam)
    )
    for i in range(3):
        drag = coef * slip[i]
        drag_ref[:, i, :] = drag
        scaled[pl.ds(i, beads, stride=8), :] = -(drag / total)

    for b in range(beads):
        eight = slice(b * 8, (b + 1) * 8)
        spread = lax.dot_general(
            scaled[eight, :].astype(bf16), w[b],
            (((1,), (1,)), ((), ())), preferred_element_type=f32,
        )
        for m in range(lists // 2):
            parts[m, eight, :] = spread[:, m * 128 : (m + 1) * 128]

    first, second = [None] * lists, [None] * lists
    for m in range(lists // 2):
        g0, g1, g2 = (parts[m, pl.ds(i, beads, stride=8), :] for i in range(3))
        first[2 * m] = jnp.where(low, g0, pltpu.roll(g1, 64, 1))
        first[2 * m + 1] = jnp.where(low, pltpu.roll(g0, 64, 1), g1)
        second[2 * m] = g2
        second[2 * m + 1] = pltpu.roll(g2, 64, 1)

    def fill(slot):
        one, two = jnp.zeros((beads, 128), f32), jnp.zeros((beads, 128), f32)
        for k in range(lists):
            here = owner_of[k] == slot
            one = jnp.where(here, first[k], one)
            two = jnp.where(here, second[k], two)
        both = jnp.concatenate([one, two], axis=1).astype(bf16)
        give[pl.ds(slot, 1)] = both.reshape(1, beads, 256)

    gives = [copy(give, got, h, d, t, give_send, give_recv) for h, d, t in to_owner]
    for c, (slot, _, _) in zip(gives, to_owner):
        fill(slot)
        c.start()
    fill(me)
    got[pl.ds(me, 1)] = give[pl.ds(me, 1)]
    arrived(give, got, give_send, give_recv, to_owner)
    summed = jnp.dot(
        asked_t[...], got[...].reshape(slots * beads, 256), preferred_element_type=f32
    )
    source_ref[...] = summed[:cells, : source_ref.shape[1]]
    for c in asks + replies + gives:
        c.wait_send()


def local(nsec, ncell, fluid, bead_vel, bead_diam, weights, tile_owner, tile_local, tile_count):
    cells_dev, width = fluid.shape
    beads, lists, cells, lanes = weights.shape
    slots = ncell + 2
    f32, bf16 = jnp.float32, jnp.bfloat16
    vmem = pl.BlockSpec(memory_space=pltpu.VMEM)
    dma = pltpu.SemaphoreType.DMA
    return pl.pallas_call(
        functools.partial(kernel, nsec, ncell),
        out_shape=(
            jax.ShapeDtypeStruct(bead_vel.shape, f32),
            jax.ShapeDtypeStruct((cells_dev, 3 * cells), f32),
        ),
        in_specs=[vmem, vmem, vmem, pl.BlockSpec(memory_space=pl.ANY), vmem, vmem, vmem],
        out_specs=(vmem, vmem),
        scratch_shapes=[
            pltpu.VMEM((beads, lists * cells, lanes), bf16),
            pltpu.VMEM((cells_dev, 384), bf16),
            pltpu.VMEM((slots, beads, 128), bf16),
            pltpu.VMEM((slots, beads, 128), bf16),
            pltpu.VMEM((128, slots * beads), bf16),
            pltpu.VMEM((slots, beads, 384), bf16),
            pltpu.VMEM((slots, beads, 384), bf16),
            pltpu.VMEM((lists // 2, beads * 8, 128), f32),
            pltpu.VMEM((beads * 8, lanes), f32),
            pltpu.VMEM((beads * 8, lanes), f32),
            pltpu.VMEM((lists // 2, beads * 8, 128), f32),
            pltpu.VMEM((slots, beads, 256), bf16),
            pltpu.VMEM((slots, beads, 256), bf16),
            dma(()),
            dma((slots,)), dma((slots,)), dma((slots,)),
            dma((slots,)), dma((slots,)), dma((slots,)),
        ],
        compiler_params=pltpu.CompilerParams(
            collective_id=0, has_side_effects=True, vmem_limit_bytes=48 * 1024 * 1024
        ),
    )(
        fluid, bead_vel, bead_diam, weights.reshape(beads, lists * cells, lanes),
        tile_owner, tile_local, tile_count.reshape(1, beads),
    )


def solution(mesh):
    both = ("sector", "cell")
    in_specs = (
        P(both, None), P(both, None, None), P(both, None), P(both, None, None, None),
        P(both, None), P(both, None), P(both),
    )
    out_specs = (P(both, None, None), P(both, None))
    body = functools.partial(local, mesh.shape["sector"], mesh.shape["cell"])
    return jax.shard_map(body, mesh=mesh, in_specs=in_specs, out_specs=out_specs, check_vma=False)
```

time: 111 us -> 31 us (0.28)
  waiting for transfers between devices: 51.8 us -> 0 us
  blocking collectives: 24.6 us -> 0 us
  Pallas kernels: 0 us -> 22.7 us
  between operations: 14.2 us -> 0.65 us
  other arithmetic: 6.96 us -> 0 us
  starting transfers between devices: 5.24 us -> 0 us
  matrix products: 4.25 us -> 0 us
  local copies, waits for them, and re-layouts: 3.61 us -> 7.24 us
    reduce_scatter x1 -> x0, waiting for transfers between devices: 48.6 us -> none  [local(): lax.psum_scatter(jnp.dot(selector, partials, precision=lax.Precision.HIGH...]
    all_gather x1 -> x0, blocking collectives: 24.6 us -> none  [local(): table = lax.all_gather(fluid, 'cell', axis=0, tiled=True)]
    pallas_call x0 -> x1, Pallas kernels: none -> 22.7 us  [local(): pl.pallas_call(functools.partial(kernel, nsec, ncell), out_shape=(jax.Sha...]
    unnamed x7 -> x12, local copies, waits for them, and re-layouts: 0.63 us -> 6.63 us
    ppermute x4 -> x0, starting transfers between devices: 5.2 us -> none  [the longest x2 3.54 us: padded(): lax.ppermute(lax.slice_in_dim(block, 0, width, axis=dim), axis, backward)]
    dot_general x4 -> x0, matrix products: 4.25 us -> none  [the longest x1 1.74 us: local(): jnp.einsum('bkcn,bjn->bkjc', weights, scaled_drag, preferred_element_type...]
    ppermute x4 -> x0, waiting for transfers between devices: 3.15 us -> none  [the longest x2 1.92 us: padded(): lax.ppermute(lax.slice_in_dim(block, block.shape[dim] - width, None, axis...]
    reduce_sum x3 -> x0, other arithmetic: 2.52 us -> none  [the longest x1 2.39 us: local(): weight_sums = jnp.sum(weights, axis=2, dtype=jnp.float32)]
  transfers between devices with their start and end apart: 5 -> 0, of which waited for: 3 -> 0; matrix products, arithmetic and copies ran while one was open for 7% -> 0% of each run, Pallas kernels for 0% -> 0%
where the time goes in v1:
time: 31 us; the launch traced here: 30.6 us
  Pallas kernels  22.7 us (73%)
  local copies, waits for them, and re-layouts  7.24 us (23%)
  between operations  0.65 us (2%)
    pallas_call x1, Pallas kernels, local(): pl.pallas_call(functools.partial(kernel, nsec, ncell), out_shape=(jax.Sha...  22.7 us
    unnamed x12, local copies, waits for them, and re-layouts  6.63 us

profile of v1, /device:TPU:0, one launch (start us, length us, event | category | flops | bytes accessed | tf_op | source)
XLA Modules:
  0.0 30.6 jit_solution(12412803434357595497)
XLA Ops:
  0.6 0.8 %copy.10.owner_ref = s32[16,8]{1,0:T(8,128)S(1)} copy(s32[16,8]{0,1:T(8,128)} %param.11) | data formatting | bytes 1024 | tf_op args[4]
  1.4 0.8 %copy.11.local_ref = s32[16,8]{1,0:T(8,128)S(1)} copy(s32[16,8]{0,1:T(8,128)} %param.12) | data formatting | bytes 1024 | tf_op args[5]
  2.1 0.8 %copy.9.vel_ref = f32[16,3,128]{2,1,0:T(4,128)S(1)} copy(f32[16,3,128]{2,0,1:T(8,128)} %param.8) | data formatting | bytes 49152 | tf_op args[1]
  2.9 0.0 copy-start
  2.9 1.6 %copy-done = bf16[16,8,64,128]{3,2,1,0:T(8,128)(2,1)S(1)} copy-done((bf16[16,8,64,128]{3,2,1,0:T(8,128)(2,1)S(1)}, bf16[16,8,64,128]{3,2,1,0:T(8,128)(2,1)}, u32[]{:S(2)}) %copy-start) | copy-done | bytes 2097176
  4.5 0.0 copy-start.1
  4.5 0.8 %copy-done.1 = bf16[64,320]{1,0:T(8,128)(2,1)S(1)} copy-done((bf16[64,320]{1,0:T(8,128)(2,1)S(1)}, bf16[64,320]{1,0:T(8,128)(2,1)}, u32[]{:S(2)}) %copy-start.1) | copy-done | bytes 40984
  5.3 0.0 copy-start.2
  5.3 0.7 %copy-done.2 = f32[16,128]{1,0:T(8,128)S(1)} copy-done((f32[16,128]{1,0:T(8,128)S(1)}, f32[16,128]{1,0:T(8,128)}, u32[]{:S(2)}) %copy-start.2) | copy-done | bytes 8216
  6.0 0.0 copy-start.3
  6.0 0.7 %copy-done.3 = s32[16]{0:T(128)S(1)} copy-done((s32[16]{0:T(128)S(1)}, s32[16]{0:T(128)}, u32[]{:S(2)}) %copy-start.3) | copy-done | bytes 88
  6.6 22.7 %shard_map.86 = (f32[16,3,128]{2,1,0:T(4,128)S(1)}, f32[64,192]{1,0:T(8,128)S(1)}) custom-call(bf16[64,320]{1,0:T(8,128)(2,1)S(1)} %copy-done.1, f32[16,3,128]{2,1,0:T(4,128)S(1)} %copy.9.vel_ref, f32[16,128]{1,0:T(8,128)S(1)} %copy-done.2, bf16[16,512,128]{2,1,0:T(8,128)(2,1)S(1)} %bitcast.2, s32[16,8]{1,0:T(8,128)S(1)} %copy.10.owner_ref, ...), custom_call_target="tpu_custom_call" | custom-call | tf_op jit(solution)/shard_map/pallas_call | solution.py:177
  29.3 0.6 %copy.12 = f32[16,3,128]{2,0,1:T(8,128)} copy(f32[16,3,128]{2,1,0:T(4,128)S(1)} %get-tuple-element.2) | data formatting | bytes 49152 | tf_op jit(solution)/shard_map/pallas_call | solution.py:177
  30.0 0.6 %copy.14 = f32[64,192]{1,0:T(8,128)} copy(f32[64,192]{1,0:T(8,128)S(1)} %get-tuple-element.7) | data formatting | bytes 98304
Async XLA Ops:
  2.9 1.6 %copy-start = (bf16[16,8,64,128]{3,2,1,0:T(8,128)(2,1)S(1)}, bf16[16,8,64,128]{3,2,1,0:T(8,128)(2,1)}, u32[]{:S(2)}) copy-start(bf16[16,8,64,128]{3,2,1,0:T(8,128)(2,1)} %param.10) | copy-start | bytes 6291460
  4.5 0.8 %copy-start.1 = (bf16[64,320]{1,0:T(8,128)(2,1)S(1)}, bf16[64,320]{1,0:T(8,128)(2,1)}, u32[]{:S(2)}) copy-start(bf16[64,320]{1,0:T(8,128)(2,1)} %fluid_ref.1) | copy-start | bytes 122884
  5.3 0.7 %copy-start.2 = (f32[16,128]{1,0:T(8,128)S(1)}, f32[16,128]{1,0:T(8,128)}, u32[]{:S(2)}) copy-start(f32[16,128]{1,0:T(8,128)} %diam_ref.1) | copy-start | bytes 24580
  6.0 0.7 %copy-start.3 = (s32[16]{0:T(128)S(1)}, s32[16]{0:T(128)}, u32[]{:S(2)}) copy-start(s32[16]{0:T(128)} %param.13) | copy-start | bytes 196

commit v2 on v1

--- a/solution.py
+++ b/solution.py
@@ -14,11 +14,11 @@
 def kernel(
     nsec, ncell, fluid_ref, vel_ref, diam_ref, weights_ref, owner_ref, local_ref, count_ref,
     drag_ref, source_ref,
+    fluid, vel, diam, owner, place, count, drags, source,
     w, table, ask, asked, asked_t, reply, rows, lhs, mixed, scaled, parts, give, got,
-    w_sem, ask_send, ask_recv, reply_send, reply_recv, give_send, give_recv,
+    in_sem, out_sem, ask_send, ask_recv, reply_send, reply_recv, give_send, give_recv,
 ):
-    lists = owner_ref.shape[1]
-    beads = owner_ref.shape[0]
+    lists, beads = owner_ref.shape
     cells = fluid_ref.shape[0]
     slots = ncell + 2
     f32, bf16 = jnp.float32, jnp.bfloat16
@@ -36,8 +36,13 @@
     for _, device, _ in to_owner:
         pl.semaphore_signal(barrier, inc=1, device_id=device, device_id_type=MESH)
 
-    load_w = pltpu.make_async_copy(weights_ref, w, w_sem)
-    load_w.start()
+    inputs = [
+        (owner_ref, owner), (local_ref, place), (count_ref, count), (fluid_ref, fluid),
+        (vel_ref, vel), (diam_ref, diam), (weights_ref, w),
+    ]
+    loads = [pltpu.make_async_copy(src, dst, in_sem.at[i]) for i, (src, dst) in enumerate(inputs)]
+    for c in loads:
+        c.start()
 
     def copy(src, dst, here, device, there, send, recv):
         return pltpu.make_async_remote_copy(
@@ -50,43 +55,47 @@
             copy(src, dst, slot, device, slot, send, recv).wait_recv()
 
     lane = lax.broadcasted_iota(jnp.int32, (beads, 128), 1)
-    square = (beads, beads)
-    diagonal = lax.broadcasted_iota(jnp.int32, square, 0) == lax.broadcasted_iota(jnp.int32, square, 1)
-    counts = jnp.broadcast_to(count_ref[...].astype(f32), square)
-    counts = jnp.sum(jnp.where(diagonal, counts, 0.0), axis=1, keepdims=True)
-    turn = lax.broadcasted_iota(jnp.int32, (beads, lists), 1).astype(f32)
-    live = turn < counts
-    keys = jnp.where(live, owner_ref[...] * 128 + local_ref[...], -1)
-    owners = jnp.where(live, owner_ref[...], -1)
-    key_of = [jnp.broadcast_to(keys[:, k : k + 1], (beads, 128)) for k in range(lists)]
-    owner_of = [jnp.broadcast_to(owners[:, k : k + 1], (beads, 128)) for k in range(lists)]
-
+    ask[...] = jnp.full_like(ask, -1.0)
+    for c in loads[:3]:
+        c.wait()
+    live = lax.broadcasted_iota(jnp.int32, (lists, beads), 0) < count[...]
+    owners = jnp.where(live, owner[...], -1).astype(f32)
+    places = place[...].astype(f32)
     for o in range(slots):
-        hit = key_of[0] == lane + o * 128
-        for k in range(1, lists):
-            hit = hit | (key_of[k] == lane + o * 128)
-        ask[o] = jnp.where(hit, 1.0, 0.0).astype(bf16)
+        ask[o, :, :beads] = jnp.max(jnp.where(owners == o, places, -1.0), axis=0, keepdims=True)
 
     pl.semaphore_wait(barrier, len(to_owner))
     asks = [copy(ask, asked, h, d, t, ask_send, ask_recv) for h, d, t in to_owner]
     for c in asks:
         c.start()
     asked[pl.ds(me, 1)] = ask[pl.ds(me, 1)]
+    diagonal = lane == lax.broadcasted_iota(jnp.int32, (beads, 128), 0)
+    lanes = lane.astype(f32)
+
+    def upright(row):
+        spread = jnp.where(diagonal[:, : row.shape[1]], jnp.broadcast_to(row, (beads, row.shape[1])), 0.0)
+        return jnp.broadcast_to(jnp.sum(spread, axis=1, keepdims=True), (beads, 128))
+
+    owner_of = [upright(owners[k : k + 1, :]) for k in range(lists)]
+    loads[3].wait()
     table[...] = jnp.ones_like(table)
-    table[:, : FIELDS * cells] = fluid_ref[...]
+    table[:, : FIELDS * cells] = fluid[...]
     lhs[...] = jnp.zeros_like(lhs)
     scaled[...] = jnp.zeros_like(scaled)
 
     arrived(ask, asked, ask_send, ask_recv, to_owner)
-    wanted = asked[...].reshape(slots * beads, 128)
-    picked = jnp.dot(wanted[:, :cells], table[...], preferred_element_type=f32)
+    wanted = jnp.concatenate(
+        [jnp.where(upright(asked[o]) == lanes, 1.0, 0.0) for o in range(slots)], axis=0
+    )
+    picked = jnp.dot(wanted.astype(bf16)[:, :cells], table[...], preferred_element_type=f32)
     reply[...] = picked.astype(bf16).reshape(reply.shape)
     replies = [copy(reply, rows, h, d, t, reply_send, reply_recv) for h, d, t in to_asker]
     for c in replies:
         c.start()
     rows[pl.ds(me, 1)] = reply[pl.ds(me, 1)]
-    asked_t[...] = wanted.astype(f32).T.astype(bf16)
-    load_w.wait()
+    asked_t[...] = wanted.T.astype(bf16)
+    for c in loads[4:]:
+        c.wait()
     arrived(reply, rows, reply_send, reply_recv, to_asker)
 
     low = lane < 64
@@ -110,22 +119,24 @@
     field = [mixed[pl.ds(f, beads, stride=8), :] for f in range(FIELDS + 1)]
     total = field[FIELDS]
     interp = [field[f] / total for f in range(FIELDS)]
-    slip = [interp[i] - vel_ref[:, i, :] for i in range(3)]
+    slip = [interp[i] - vel[i] for i in range(3)]
     porosity, viscosity = interp[3], interp[4]
-    diam = diam_ref[...]
+    across = diam[...]
     speed = jnp.sqrt(slip[0] * slip[0] + slip[1] * slip[1] + slip[2] * slip[2] + 0.01)
-    reynolds = porosity * diam * speed / viscosity
+    reynolds = porosity * across * speed / viscosity
     coef = (
         viscosity
         * (1.0 + 0.15 * jnp.exp(0.687 * jnp.log(reynolds)))
         * jnp.exp(-1.65 * jnp.log(porosity))
-        / (diam * diam)
+        / (across * across)
     )
     for i in range(3):
         drag = coef * slip[i]
-        drag_ref[:, i, :] = drag
+        drags[i] = drag
         scaled[pl.ds(i, beads, stride=8), :] = -(drag / total)
 
+    store_drag = pltpu.make_async_copy(drags, drag_ref, out_sem.at[0])
+    store_drag.start()
     for b in range(beads):
         eight = slice(b * 8, (b + 1) * 8)
         spread = lax.dot_general(
@@ -162,31 +173,43 @@
     summed = jnp.dot(
         asked_t[...], got[...].reshape(slots * beads, 256), preferred_element_type=f32
     )
-    source_ref[...] = summed[:cells, : source_ref.shape[1]]
+    source[...] = summed[:cells, : source_ref.shape[1]]
+    store_source = pltpu.make_async_copy(source, source_ref, out_sem.at[1])
+    store_source.start()
     for c in asks + replies + gives:
         c.wait_send()
+    store_drag.wait()
+    store_source.wait()
 
 
 def local(nsec, ncell, fluid, bead_vel, bead_diam, weights, tile_owner, tile_local, tile_count):
     cells_dev, width = fluid.shape
     beads, lists, cells, lanes = weights.shape
     slots = ncell + 2
-    f32, bf16 = jnp.float32, jnp.bfloat16
-    vmem = pl.BlockSpec(memory_space=pltpu.VMEM)
+    f32, bf16, i32 = jnp.float32, jnp.bfloat16, jnp.int32
+    hbm = pl.BlockSpec(memory_space=pltpu.HBM)
     dma = pltpu.SemaphoreType.DMA
-    return pl.pallas_call(
+    drag, source = pl.pallas_call(
         functools.partial(kernel, nsec, ncell),
         out_shape=(
-            jax.ShapeDtypeStruct(bead_vel.shape, f32),
+            jax.ShapeDtypeStruct((3, beads, lanes), f32),
             jax.ShapeDtypeStruct((cells_dev, 3 * cells), f32),
         ),
-        in_specs=[vmem, vmem, vmem, pl.BlockSpec(memory_space=pl.ANY), vmem, vmem, vmem],
-        out_specs=(vmem, vmem),
+        in_specs=[hbm] * 7,
+        out_specs=(hbm, hbm),
         scratch_shapes=[
+            pltpu.VMEM((cells_dev, width), bf16),
+            pltpu.VMEM((3, beads, lanes), f32),
+            pltpu.VMEM((beads, lanes), f32),
+            pltpu.VMEM((lists, beads), i32),
+            pltpu.VMEM((lists, beads), i32),
+            pltpu.VMEM((1, beads), i32),
+            pltpu.VMEM((3, beads, lanes), f32),
+            pltpu.VMEM((cells_dev, 3 * cells), f32),
             pltpu.VMEM((beads, lists * cells, lanes), bf16),
             pltpu.VMEM((cells_dev, 384), bf16),
-            pltpu.VMEM((slots, beads, 128), bf16),
-            pltpu.VMEM((slots, beads, 128), bf16),
+            pltpu.VMEM((slots, 1, 128), f32),
+            pltpu.VMEM((slots, 1, 128), f32),
             pltpu.VMEM((128, slots * beads), bf16),
             pltpu.VMEM((slots, beads, 384), bf16),
             pltpu.VMEM((slots, beads, 384), bf16),
@@ -196,17 +219,19 @@
             pltpu.VMEM((lists // 2, beads * 8, 128), f32),
             pltpu.VMEM((slots, beads, 256), bf16),
             pltpu.VMEM((slots, beads, 256), bf16),
-            dma(()),
+            dma((7,)), dma((2,)),
             dma((slots,)), dma((slots,)), dma((slots,)),
             dma((slots,)), dma((slots,)), dma((slots,)),
         ],
         compiler_params=pltpu.CompilerParams(
-            collective_id=0, has_side_effects=True, vmem_limit_bytes=48 * 1024 * 1024
+            collective_id=0, has_side_effects=True, vmem_limit_bytes=60 * 1024 * 1024
         ),
     )(
-        fluid, bead_vel, bead_diam, weights.reshape(beads, lists * cells, lanes),
-        tile_owner, tile_local, tile_count.reshape(1, beads),
-    )
+        fluid, bead_vel.transpose(1, 0, 2), bead_diam,
+        weights.reshape(beads, lists * cells, lanes),
+        tile_owner.T, tile_local.T, tile_count.reshape(1, beads),
+    )
+    return drag.transpose(1, 0, 2), source
 
 
 def solution(mesh):

time: 31 us -> 26.6 us (0.86)
  local copies, waits for them, and re-layouts: 7.24 us -> 2.82 us
    unnamed x12 -> x2, local copies, waits for them, and re-layouts: 6.63 us -> 2.82 us
    pallas_call x1 -> x0, local copies, waits for them, and re-layouts: 0.61 us -> none  [local(): pl.pallas_call(functools.partial(kernel, nsec, ncell), out_shape=(jax.Sha...]
where the time goes in v2:
time: 26.6 us; the launch traced here: 26.4 us
  Pallas kernels  22.9 us (86%)
  local copies, waits for them, and re-layouts  2.82 us (11%)
  between operations  0.64 us (2%)
    pallas_call x1, Pallas kernels, local(): pl.pallas_call(functools.partial(kernel, nsec, ncell), out_shape=(jax.Sha...  22.9 us
    unnamed x2, local copies, waits for them, and re-layouts  2.82 us

profile of v2, /device:TPU:0, one launch (start us, length us, event | category | flops | bytes accessed | tf_op | source)
XLA Modules:
  0.0 26.4 jit_solution(2315964718075500554)
XLA Ops:
  0.6 22.9 %shard_map.86 = (f32[3,16,128]{2,1,0:T(8,128)}, f32[64,192]{1,0:T(8,128)}) custom-call(bf16[64,320]{1,0:T(8,128)(2,1)} %fluid_ref.1, f32[3,16,128]{2,1,0:T(8,128)} %bitcast.7, f32[16,128]{1,0:T(8,128)} %diam_ref.1, bf16[16,512,128]{2,1,0:T(8,128)(2,1)} %bitcast.6, s32[8,16]{1,0:T(8,128)} %bitcast.9, s32[8,16]{1,0:T(8,128)} %bitcast.10, s32[1,16]{1,0:T(1,128)} %bitcast.11), custom_call_target="tpu_custom_call" | custom-call | tf_op jit(solution)/shard_map/pallas_call | solution.py:192
  23.6 1.3 %copy.11 = f32[16,3,128]{2,0,1:T(8,128)} copy(f32[16,3,128]{2,0,1:T(8,128)} %bitcast.8) | data formatting | bytes 49152
  24.9 1.5 %copy.12 = f32[64,192]{1,0:T(8,128)} copy(f32[64,192]{1,0:T(8,128)} %get-tuple-element.9) | data formatting | bytes 98304

commit v3 on v2

--- a/solution.py
+++ b/solution.py
@@ -182,12 +182,18 @@
     store_source.wait()
 
 
+def hand_over(drag_ref, source_ref, drag_out, source_out):
+    drag_out[...] = drag_ref[...]
+    source_out[...] = source_ref[...]
+
+
 def local(nsec, ncell, fluid, bead_vel, bead_diam, weights, tile_owner, tile_local, tile_count):
     cells_dev, width = fluid.shape
     beads, lists, cells, lanes = weights.shape
     slots = ncell + 2
     f32, bf16, i32 = jnp.float32, jnp.bfloat16, jnp.int32
     hbm = pl.BlockSpec(memory_space=pltpu.HBM)
+    vmem = pl.BlockSpec(memory_space=pltpu.VMEM)
     dma = pltpu.SemaphoreType.DMA
     drag, source = pl.pallas_call(
         functools.partial(kernel, nsec, ncell),
@@ -231,6 +237,15 @@
         weights.reshape(beads, lists * cells, lanes),
         tile_owner.T, tile_local.T, tile_count.reshape(1, beads),
     )
+    drag, source = pl.pallas_call(
+        hand_over,
+        out_shape=(
+            jax.ShapeDtypeStruct(drag.shape, f32), jax.ShapeDtypeStruct(source.shape, f32),
+        ),
+        in_specs=[vmem] * 2,
+        out_specs=(vmem, vmem),
+        compiler_params=pltpu.CompilerParams(vmem_limit_bytes=60 * 1024 * 1024),
+    )(drag, source)
     return drag.transpose(1, 0, 2), source
 
 

time: 26.6 us -> 25.2 us (0.947)
  local copies, waits for them, and re-layouts: 2.82 us -> 0 us
  Pallas kernels: 22.9 us -> 24.4 us
    unnamed x2 -> x0, local copies, waits for them, and re-layouts: 2.82 us -> none
    pallas_call x0 -> x1, Pallas kernels: none -> 1.5 us  [local(): pl.pallas_call(hand_over, out_shape=(jax.ShapeDtypeStruct(drag.shape, f32...]
where the time goes in v3:
time: 25.2 us; the launch traced here: 25 us
  Pallas kernels  24.4 us (97%)
  between operations  0.64 us (3%)
    pallas_call x1, Pallas kernels, local(): pl.pallas_call(functools.partial(kernel, nsec, ncell), out_shape=(jax.Sha...  22.9 us
    pallas_call x1, Pallas kernels, local(): pl.pallas_call(hand_over, out_shape=(jax.ShapeDtypeStruct(drag.shape, f32...  1.5 us

profile of v3, /device:TPU:0, one launch (start us, length us, event | category | flops | bytes accessed | tf_op | source)
XLA Modules:
  0.0 25.0 jit_solution(13169394804910474839)
XLA Ops:
  0.6 22.9 %shard_map.86 = (f32[3,16,128]{2,1,0:T(8,128)}, f32[64,192]{1,0:T(8,128)}) custom-call(bf16[64,320]{1,0:T(8,128)(2,1)} %fluid_ref.1, f32[3,16,128]{2,1,0:T(8,128)} %bitcast.7, f32[16,128]{1,0:T(8,128)} %diam_ref.1, bf16[16,512,128]{2,1,0:T(8,128)(2,1)} %bitcast.6, s32[8,16]{1,0:T(8,128)} %bitcast.8, s32[8,16]{1,0:T(8,128)} %bitcast.9, s32[1,16]{1,0:T(1,128)} %bitcast.10), custom_call_target="tpu_custom_call" | custom-call | tf_op jit(solution)/shard_map/pallas_call | solution.py:198
  23.5 1.5 %shard_map.87 = (f32[3,16,128]{2,1,0:T(8,128)}, f32[64,192]{1,0:T(8,128)}) custom-call(f32[3,16,128]{2,1,0:T(8,128)} %get-tuple-element.6.drag_ref, f32[64,192]{1,0:T(8,128)} %get-tuple-element.7.source_ref), custom_call_target="tpu_custom_call" | custom-call | tf_op jit(solution)/shard_map/pallas_call | solution.py:240

commit v4 on v3

--- a/solution.py
+++ b/solution.py
@@ -83,16 +83,34 @@
     lhs[...] = jnp.zeros_like(lhs)
     scaled[...] = jnp.zeros_like(scaled)
 
-    arrived(ask, asked, ask_send, ask_recv, to_owner)
+    behind = [lax.rem(me + ncell - t, ncell) for t in range(1, ncell)]
+    near = [(o, {"cell": o}, me) for o in behind[: ncell // 2]]
+    far = [(o, {"cell": o}, me) for o in behind[ncell // 2 :]]
+    rim = [(ncell, succ, ncell), (ncell + 1, prev, ncell + 1)]
+
+    def answer(links, own):
+        arrived(ask, asked, ask_send, ask_recv, links)
+        froms = own + [slot for slot, _, _ in links]
+        sought = jnp.concatenate(
+            [jnp.where(upright(asked[o]) == lanes, 1.0, 0.0) for o in froms], axis=0
+        )
+        picked = jnp.dot(sought.astype(bf16)[:, :cells], table[...], preferred_element_type=f32)
+        picked = picked.astype(bf16)
+        sent = []
+        for n, slot in enumerate(froms):
+            block = picked[n * beads : (n + 1) * beads].reshape(1, beads, 384)
+            reply[pl.ds(slot, 1)] = block
+            if n >= len(own):
+                _, device, there = links[n - len(own)]
+                sent.append(copy(reply, rows, slot, device, there, reply_send, reply_recv))
+                sent[-1].start()
+        return sent
+
+    replies = answer(near + rim, [me]) + answer(far, [])
+    rows[pl.ds(me, 1)] = reply[pl.ds(me, 1)]
     wanted = jnp.concatenate(
         [jnp.where(upright(asked[o]) == lanes, 1.0, 0.0) for o in range(slots)], axis=0
     )
-    picked = jnp.dot(wanted.astype(bf16)[:, :cells], table[...], preferred_element_type=f32)
-    reply[...] = picked.astype(bf16).reshape(reply.shape)
-    replies = [copy(reply, rows, h, d, t, reply_send, reply_recv) for h, d, t in to_asker]
-    for c in replies:
-        c.start()
-    rows[pl.ds(me, 1)] = reply[pl.ds(me, 1)]
     asked_t[...] = wanted.T.astype(bf16)
     for c in loads[4:]:
         c.wait()

time: 25.2 us -> 25.1 us (level)
  no operation moved by 1% of the time
where the time goes in v4:
time: 25.1 us; the launch traced here: 24.9 us
  Pallas kernels  24.3 us (97%)
  between operations  0.64 us (3%)
    pallas_call x1, Pallas kernels, local(): pl.pallas_call(functools.partial(kernel, nsec, ncell), out_shape=(jax.Sha...  22.8 us
    pallas_call x1, Pallas kernels, local(): pl.pallas_call(hand_over, out_shape=(jax.ShapeDtypeStruct(drag.shape, f32...  1.5 us

profile of v4, /device:TPU:0, one launch (start us, length us, event | category | flops | bytes accessed | tf_op | source)
XLA Modules:
  0.0 24.9 jit_solution(4003204185105466043)
XLA Ops:
  0.6 22.8 %shard_map.86 = (f32[3,16,128]{2,1,0:T(8,128)}, f32[64,192]{1,0:T(8,128)}) custom-call(bf16[64,320]{1,0:T(8,128)(2,1)} %fluid_ref.1, f32[3,16,128]{2,1,0:T(8,128)} %bitcast.7, f32[16,128]{1,0:T(8,128)} %diam_ref.1, bf16[16,512,128]{2,1,0:T(8,128)(2,1)} %bitcast.6, s32[8,16]{1,0:T(8,128)} %bitcast.8, s32[8,16]{1,0:T(8,128)} %bitcast.9, s32[1,16]{1,0:T(1,128)} %bitcast.10), custom_call_target="tpu_custom_call" | custom-call | tf_op jit(solution)/shard_map/pallas_call | solution.py:216
  23.4 1.5 %shard_map.87 = (f32[3,16,128]{2,1,0:T(8,128)}, f32[64,192]{1,0:T(8,128)}) custom-call(f32[3,16,128]{2,1,0:T(8,128)} %get-tuple-element.6.drag_ref, f32[64,192]{1,0:T(8,128)} %get-tuple-element.7.source_ref), custom_call_target="tpu_custom_call" | custom-call | tf_op jit(solution)/shard_map/pallas_call | solution.py:258
